TPU v7x, 128 devices: a whole 4x4x4 slice. The times are simulated.
128 devices in a mesh: blk: 32 (over z, x_hi, y), layer: 4 (over x_lo, core).
Axes of the slice: x: 4 (x_hi: 2, x_lo: 2; x = x_hi * 2 + x_lo), y: 4, z: 4, core: 2. Of those that a mesh axis runs over, the one named last changes fastest.
Arguments:
- density: float32 [32768, 3, 1024], P('blk', None, 'layer'), may hold values from -0.80592746 to 0.80592746
- tile_mask: int32 [256, 3, 8], P('blk', None, 'layer'), may hold values 0 or 1
Outputs:
- squared: float32 [32768, 5, 1024], P('blk', None, 'layer')
All inputs are finite; a program needn't handle non-finite values. No bound on the sum of `tile_mask` on one device may be relied on, other than what follows from the above.
Results may differ from a plain program's by a relative error of at most 0.0003.
Values sent between devices are 32-bit elements; how exact they have to be, the bound alone decides.
A program may use at most 128 MiB of HBM per device.

v0:
```python
import jax
import jax.numpy as jnp
from jax import lax
from jax.sharding import PartitionSpec as P

TILE = 128


def passed_along(shard, axis, by):
    devices = lax.axis_size(axis)
    return lax.ppermute(shard, axis, [(i, (i + by) % devices) for i in range(devices)])


def neighbours(panel):
    following = passed_along(panel, "blk", -1)
    preceding = passed_along(following, "blk", 2)
    return (preceding, following)


def band_product(left, panels, cols):
    rows = left.shape[0]
    result = jnp.zeros((rows, 5, cols), jnp.float32)
    for offset in range(3):
        other = panels[offset]
        flat = other.reshape(other.shape[0], 3 * cols)
        term = jnp.dot(
            left[:, offset, :],
            flat,
            preferred_element_type=jnp.float32,
            precision=lax.Precision.HIGHEST,
        )
        result = result.at[:, offset : offset + 3, :].add(term.reshape(rows, 3, cols))
    return result


def local(density, tile_mask):
    rows = density.shape[0]
    quarter = density.shape[2]
    tile_rows = tile_mask.shape[0]
    tile_cols = tile_mask.shape[2]
    masked = (
        density.reshape(tile_rows, TILE, 3, tile_cols, TILE)
        * tile_mask.astype(jnp.float32)[:, None, :, :, None]
    )
    kept = masked.reshape(rows, 3, quarter)
    own_panel = lax.all_to_all(kept, "layer", split_axis=0, concat_axis=2, tiled=True)
    preceding, following = neighbours(own_panel)
    partial_value = band_product(kept, (preceding, own_panel, following), own_panel.shape[2])
    return lax.psum_scatter(partial_value, "layer", scatter_dimension=2, tiled=True)


def solution(mesh):
    placed = (P("blk", None, "layer"), P("blk", None, "layer"))
    return jax.shard_map(
        local, mesh=mesh, in_specs=placed, out_specs=P("blk", None, "layer"), check_vma=False
    )
```

profile of v0, /device:TPU:0, one launch (start us, length us, event | category | flops | bytes accessed | tf_op | source)
XLA Modules:
  0.0 457.7 jit_solution(17642721988149951957)
XLA Ops:
  6.5 0.0 reduce-scatter.2.cloned.1.call-start
  6.5 0.7 convert_element_type.3
  7.2 0.1 copy.8
  7.3 0.9 mul.11
  8.2 3.6 mul.12
  11.8 3.2 mul.13
  15.1 2.2 copy.9
  17.3 50.8 %all_to_all.18 = f32[1024,3,256]{2,1,0:T(4,128)S(1)} all-to-all(f32[1024,3,256]{2,1,0:T(4,128)S(1)} %copy.9), channel_id=1, replica_groups=mesh['blk'=32,'layer'=4] {'layer'}, dimensions={0} | all-to-all | bytes 6291456 | tf_op jit(solution)/shard_map/all_to_all | solution.py:46
  68.1 2.2 copy.10
  70.3 3.5 copy.11
  73.8 8.9 %collective-permute-start = (f32[256,3,1024]{0,2,1:T(8,128)}, f32[256,3,1024]{0,2,1:T(8,128)S(1)}, u32[]{:S(2)}, u32[]{:S(2)}) collective-permute-start(f32[256,3,1024]{0,2,1:T(8,128)} %bitcast.42), channel_id=1, source_target_pairs={{0,124},{4,0},{8,4},{12,8},{16,12},{20,16},{24,20},{28,24},{32,28}... | collective-permute-start | bytes 9437192 | tf_op jit(solution)/shard_map/ppermute | solution.py:11
  82.8 67.3 %collective-permute-done = f32[256,3,1024]{0,2,1:T(8,128)S(1)} collective-permute-done((f32[256,3,1024]{0,2,1:T(8,128)}, f32[256,3,1024]{0,2,1:T(8,128)S(1)}, u32[]{:S(2)}, u32[]{:S(2)}) %collective-permute-start) | collective-permute-done | bytes 3145760 | tf_op jit(solution)/shard_map/ppermute | solution.py:11
  150.1 0.0 collective-permute-start.1
  150.1 74.6 %collective-permute-done.1 = f32[256,3,1024]{0,2,1:T(8,128)S(1)} collective-permute-done((f32[256,3,1024]{0,2,1:T(8,128)S(1)}, f32[256,3,1024]{0,2,1:T(8,128)S(1)}, u32[]{:S(2)}, u32[]{:S(2)}) %collective-permute-start.1) | collective-permute-done | bytes 3145760 | tf_op jit(solution)/shard_map/ppermute | solution.py:11
  224.7 11.2 %fusion.5 = f32[1024,3,1024]{2,0,1:T(8,128)S(1)} fusion(f32[256,3,1024]{0,2,1:T(8,128)S(1)} %collective-permute-done.1, f32[1024,3,256]{2,0,1:T(8,128)S(1)} %mul.13), kind=kOutput, calls=%fused_computation.5 | convolution fusion | flops 9663676416 | bytes 16777216 | tf_op jit(solution)/shard_map/dot_general | solution.py:26
  235.9 0.0 copy-start
  235.9 7.8 %scatter-add.10 = f32[1024,5,1024]{2,0,1:T(8,128)} pad(f32[1024,3,1024]{2,0,1:T(8,128)S(1)} %fusion.5, f32[]{:T(128)} %constant.80.clone.1), padding=0_0x0_2x0_0 | pad | bytes 33554436 | tf_op jit(solution)/shard_map/scatter-add | solution.py:32
  243.7 0.0 copy-done
  243.7 15.0 %add_dynamic-update-slice_fusion = f32[1024,5,1024]{2,0,1:T(8,128)} fusion(f32[1024,5,1024]{2,0,1:T(8,128)} %scatter-add.10, f32[3,1024,256]{2,1,0:T(8,128)S(1)} %bitcast.43, f32[1024,3,256]{2,0,1:T(8,128)S(1)} %mul.13), kind=kOutput, calls=%fused_computation.2 | convolution fusion | flops 9666822144 | bytes 29360128 | tf_op jit(solution)/shard_map/dot_general | solution.py:26
  258.7 14.9 %fusion = f32[1024,5,1024]{2,0,1:T(8,128)} fusion(f32[1024,5,1024]{2,0,1:T(8,128)} %add_dynamic-update-slice_fusion, f32[256,3,1024]{0,2,1:T(8,128)S(1)} %collective-permute-done, f32[1024,3,256]{2,0,1:T(8,128)S(1)} %mul.13), kind=kOutput, calls=%fused_computation.1 | convolution fusion | flops 9666822144 | bytes 29360128 | tf_op jit(solution)/shard_map/dot_general | solution.py:26
  273.6 0.0 reduce-scatter.2.cloned.1.call-update
  273.6 177.2 %reduce-scatter.2.cloned.1.call-done = f32[1024,5,256]{2,0,1:T(8,128)} async-done(((f32[1024,5,1024]{2,0,1:T(8,128)}), f32[1024,5,256]{2,0,1:T(8,128)}) %reduce-scatter.2.cloned.1.call-update) | async-done | bytes 5242896 | tf_op jit(solution)/shard_map/reduce_scatter | solution.py:49
Async XLA Ops:
  6.5 444.3 %reduce-scatter.2.cloned.1.call-start = ((), (), s32[]{:S(2)}) async-start(), calls=%async_computation.2 | async-start | bytes 26214400 | tf_op jit(solution)/shard_map/reduce_scatter | solution.py:49
  73.8 76.3 %collective-permute-start = (f32[256,3,1024]{0,2,1:T(8,128)}, f32[256,3,1024]{0,2,1:T(8,128)S(1)}, u32[]{:S(2)}, u32[]{:S(2)}) collective-permute-start(f32[256,3,1024]{0,2,1:T(8,128)} %bitcast.42), channel_id=1, source_target_pairs={{0,124},{4,0},{8,4},{12,8},{16,12},{20,16},{24,20},{28,24},{32,28}... | collective-permute-start | bytes 9437192 | tf_op jit(solution)/shard_map/ppermute | solution.py:11
  150.1 74.6 %collective-permute-start.1 = (f32[256,3,1024]{0,2,1:T(8,128)S(1)}, f32[256,3,1024]{0,2,1:T(8,128)S(1)}, u32[]{:S(2)}, u32[]{:S(2)}) collective-permute-start(f32[256,3,1024]{0,2,1:T(8,128)S(1)} %collective-permute-done), channel_id=1, source_target_pairs={{0,8},{4,12},{8,16},{12,20},{16,24},{20,28},{24,32},{28,36},{32,40... | collective-permute-start | bytes 9437192 | tf_op jit(solution)/shard_map/ppermute | solution.py:11
  235.9 7.8 %copy-start = (f32[256,3,4,256]{0,3,2,1:T(8,128)S(1)}, f32[256,3,4,256]{0,3,2,1:T(8,128)}, u32[]{:S(2)}) copy-start(f32[256,3,4,256]{0,3,2,1:T(8,128)} %copy.11) | copy-start | bytes 9437188
Sparse Core Ops, SparseCore 0:
  273.8 177.0 reduce-scatter.1
where the time goes:
time: 459 us; the launch traced here: 458 us
  waiting for transfers between devices  319 us (69%)
  blocking collectives  50.8 us (11%)
  matrix products  41.1 us (9%)
  local copies, waits for them, and re-layouts  20.3 us (4%)
  between operations  13.4 us (3%)
  starting transfers between devices  8.95 us (2%)
    reduce_scatter x1, waiting for transfers between devices, local(): lax.psum_scatter(partial_value, 'layer', scatter_dimension=2, tiled=True)  177 us
    ppermute x2, waiting for transfers between devices, passed_along(): lax.ppermute(shard, axis, [(i, (i + by) % devices) for i in range(devices)])  142 us
    all_to_all x1, blocking collectives, local(): lax.all_to_all(kept, 'layer', split_axis=0, concat_axis=2, tiled=True)  50.8 us
    dot_general x3, matrix products, band_product(): jnp.dot(left[:, offset, :], flat, preferred_element_type=jnp.float32, pre...  41.1 us
  transfers between devices with their start and end apart: 3, of which 3 were waited for; matrix products, arithmetic and copies ran while one was open for 0% of the time, Pallas kernels for 0%

commit v1 on v0

v1 whole, which is shorter than its diff:
```python
import functools

import jax
import jax.numpy as jnp
from jax import lax
from jax.experimental import pallas as pl
from jax.experimental.pallas import tpu as pltpu
from jax.sharding import PartitionSpec as P

TILE = 128
Q = 256
SUB = 64
NSUB = Q // SUB
Y = 4
F32 = jnp.float32
BF16 = jnp.bfloat16
MESH = pl.DeviceIdType.MESH
BLOCKS = [(rho, b) for rho in range(4) for b in range(3)]


def kernel(
    dens, mask, out, own, sib, par, fwd, pre, fol, lh, ll, rh, rl,
    load_sem, sib_send, sib_recv, par_send, par_recv, fwd_send, fwd_recv,
    nxt_send, pre_recv, prv_send, fol_recv,
):
    blk = lax.axis_index("blk")
    lay = lax.axis_index("layer")
    nblk = lax.axis_size("blk")
    half = lay // 2
    core = lay % 2
    y = lax.rem(blk, Y)
    at_end = y == Y - 1
    at_start = y == 0
    other_half = (1 - half) * 2 + core
    partner = (blk, other_half)
    sibling = (blk, half * 2 + 1 - core)
    nxt = (lax.rem(blk + 1, nblk), jnp.where(at_end, other_half, lay))
    prv = (lax.rem(blk + nblk - 1, nblk), jnp.where(at_start, other_half, lay))

    def row_of(rho):
        return pl.multiple_of(lax.rem(2 * half + rho, 4) * Q, Q)

    def par_row_of(rho):
        return pl.multiple_of(lax.rem(2 * half + 2 + rho, 4) * Q, Q)

    def remote(src, dst, send, recv, to):
        return pltpu.make_async_remote_copy(
            src_ref=src, dst_ref=dst, send_sem=send, recv_sem=recv,
            device_id=to, device_id_type=MESH,
        )

    def load(k, rho, b):
        rows = pl.ds(row_of(rho), Q)
        return pltpu.make_async_copy(dens.at[b, rows], own.at[b, rows], load_sem.at[k])

    def to_sibling(k, rho, b):
        rows = pl.ds(row_of(rho), Q)
        return remote(own.at[b, rows], sib.at[b, rows], sib_send.at[k], sib_recv.at[k], sibling)

    def to_partner(k, rho, b, s):
        rows = pl.ds(row_of(rho) + s * SUB, SUB)
        return remote(own.at[b, rows], par.at[b, rows], par_send.at[k], par_recv.at[k, s], partner)

    def block_to_next(k, rho, b):
        rows = pl.ds(row_of(rho), Q)
        return remote(own.at[b, rows], pre.at[b, rows], nxt_send.at[k], pre_recv.at[k], nxt)

    def block_to_prev(k, rho, b):
        rows = pl.ds(row_of(rho), Q)
        return remote(own.at[b, rows], fol.at[b, rows], prv_send.at[k], fol_recv.at[k], prv)

    def send_block(k):
        rho, b = BLOCKS[k]
        for s in range(NSUB):
            to_partner(k, rho, b, s).start()

        @pl.when(jnp.logical_not(at_end))
        def _():
            block_to_next(k, rho, b).start()

        @pl.when(jnp.logical_not(at_start))
        def _():
            block_to_prev(k, rho, b).start()

    def forward(k, s):
        rho, b = BLOCKS[k]
        rows = pl.ds(par_row_of(rho) + s * SUB, SUB)
        remote(own.at[b, rows], par.at[b, rows], par_send.at[k], par_recv.at[k, s], partner).wait_recv()
        remote(par.at[b, rows], fwd.at[b, rows], fwd_send.at[k], fwd_recv.at[k], sibling).start()

        @pl.when(at_end)
        def _():
            remote(par.at[b, rows], pre.at[b, rows], nxt_send.at[k], pre_recv.at[k], nxt).start()

        @pl.when(at_start)
        def _():
            remote(par.at[b, rows], fol.at[b, rows], prv_send.at[k], fol_recv.at[k], prv).start()

    def split(x):
        hi = x.astype(BF16)
        return hi, (x - hi.astype(F32)).astype(BF16)

    def keep_left(slot, o, r0, n, x):
        hi, lo = split(x)
        lh[slot, o, pl.ds(r0, n), :] = hi
        ll[slot, o, pl.ds(r0, n), :] = lo

    def mask_own(rho, b):
        r0 = row_of(rho)
        t0 = lax.rem(2 * half + rho, 4) * 2
        for t in range(2):
            for j in range(2):
                m = mask[b, j, t0 + t].astype(F32)
                rows = pl.ds(r0 + t * TILE, TILE)
                cols = pl.ds(j * TILE, TILE)
                x = own[b, rows, cols] * m
                own[b, rows, cols] = x
                hi, lo = split(x)
                lh[core, b, rows, cols] = hi
                ll[core, b, rows, cols] = lo

    def product(o, b, rho, r0, n):
        rows = pl.ds(r0, n)
        ah = lh[rho, o, rows, :]
        al = ll[rho, o, rows, :]
        if o == 1:
            inner = pl.ds(row_of(rho), Q)
            wh = lh[core, b, inner, :]
            wl = ll[core, b, inner, :]
        else:
            wh = rh[o // 2, rho, b]
            wl = rl[o // 2, rho, b]
        dot = functools.partial(jnp.dot, preferred_element_type=F32)
        out[o + b, rows, :] += dot(ah, wh) + dot(ah, wl) + dot(al, wh)

    def arrive(k):
        rho, b = BLOCKS[k]
        prow = par_row_of(rho)
        rows = pl.ds(prow, Q)
        keep_left(2 + core, b, prow, Q, par[b, rows, :])
        remote(par.at[b, rows], fwd.at[b, rows], fwd_send.at[k], fwd_recv.at[k], sibling).wait_recv()
        keep_left(3 - core, b, prow, Q, fwd[b, rows, :])
        krows = pl.ds(row_of(rho), Q)
        block_to_next(k, rho, b).wait_recv()
        hi, lo = split(pre[b, krows, :])
        rh[0, rho, b] = hi
        rl[0, rho, b] = lo
        block_to_prev(k, rho, b).wait_recv()
        hi, lo = split(fol[b, krows, :])
        rh[1, rho, b] = hi
        rl[1, rho, b] = lo

    first = pl.multiple_of((1 - half) * 2 * Q, 2 * Q)

    def work(k):
        rho, b = BLOCKS[k]
        third, fourth = par_row_of(2), par_row_of(3)
        todo = [functools.partial(arrive, k)]

        def add(*what):
            todo.append(functools.partial(product, *what))

        if rho < 2:
            for o in (0, 2):
                add(o, b, rho, 0, 4 * Q)
        else:
            for o in (0, 2):
                have = 3 * (rho - 2) + b - o
                if have >= 3:
                    add(o, b, rho, 0, 4 * Q)
                else:
                    add(o, b, rho, first, 2 * Q)
                    if have >= 0:
                        add(o, b, rho, third, Q)
            if b != 1:
                rows = third if rho == 2 else fourth
                for r in (2, 3):
                    for c in range(3):
                        if 3 * r + c < k:
                            add(b, c, r, rows, Q)
        if b == 1:
            for c in range(3):
                for r in (2, 3):
                    add(1, c, r, par_row_of(rho), Q)
        return todo

    for k, (rho, b) in enumerate(BLOCKS):
        load(k, rho, b).start()
    barrier = pltpu.get_barrier_semaphore()
    for device in (partner, sibling, nxt, prv):
        pl.semaphore_signal(barrier, inc=1, device_id=device, device_id_type=MESH)
    for k in range(2):
        load(k, *BLOCKS[k]).wait()
        mask_own(*BLOCKS[k])
    pl.semaphore_wait(barrier, 4)
    for k in range(2):
        send_block(k)
        to_sibling(k, *BLOCKS[k]).start()
    for k in range(2, 12):
        load(k, *BLOCKS[k]).wait()
        mask_own(*BLOCKS[k])
        to_sibling(k, *BLOCKS[k]).start()
    for j in range(5):
        out[j] = jnp.zeros_like(out[j])

    def sib_block(k):
        rho, b = BLOCKS[k]
        to_sibling(k, rho, b).wait_recv()
        rows = pl.ds(row_of(rho), Q)
        keep_left(1 - core, b, row_of(rho), Q, sib[b, rows, :])

    queue = [(0, functools.partial(sib_block, k)) for k in range(12)]
    queue += [(0, functools.partial(product, 1, b, r, 0, 4 * Q)) for b in range(3) for r in range(2)]
    for k in range(12):
        queue += [(min(NSUB * (k + 1) + 1, 12 * NSUB - 1) if k < 11 else 12 * NSUB, t) for t in work(k)]
    at = 0
    for s in range(12 * NSUB):
        k, piece = divmod(s, NSUB)
        if piece == 0 and k + 2 < 12:
            send_block(k + 2)
        forward(k, piece)
        done = 0
        limit = 4 if s < 12 * NSUB - 4 else 3
        while at < len(queue) and queue[at][0] <= s and done < limit:
            queue[at][1]()
            at += 1
            done += 1
    for _, thunk in queue[at:]:
        thunk()

    for k, (rho, b) in enumerate(BLOCKS):
        rows = pl.ds(row_of(rho), Q)
        prow = pl.ds(par_row_of(rho), Q)
        to_sibling(k, rho, b).wait_send()
        remote(own.at[b, rows], par.at[b, rows], par_send.at[k], par_recv.at[k, 0], partner).wait_send()
        remote(par.at[b, prow], fwd.at[b, prow], fwd_send.at[k], fwd_recv.at[k], sibling).wait_send()
        block_to_next(k, rho, b).wait_send()
        block_to_prev(k, rho, b).wait_send()


def local(density, tile_mask):
    dens = jnp.transpose(density, (1, 0, 2))
    mask = jnp.transpose(tile_mask, (1, 2, 0))
    panel = pltpu.VMEM(dens.shape, F32)
    dma = pltpu.SemaphoreType.DMA
    rows, cols = dens.shape[1:]
    out = pl.pallas_call(
        kernel,
        out_shape=jax.ShapeDtypeStruct((5, rows, cols), F32),
        in_specs=[pl.BlockSpec(memory_space=pl.ANY), pl.BlockSpec(memory_space=pltpu.SMEM)],
        out_specs=pl.BlockSpec(memory_space=pltpu.VMEM),
        scratch_shapes=[panel] * 6
        + [pltpu.VMEM((4, 3, rows, cols), BF16)] * 2
        + [pltpu.VMEM((2, 4, 3, Q, cols), BF16)] * 2
        + [dma((12,))] * 4
        + [dma((12, NSUB))]
        + [dma((12,))] * 6,
        compiler_params=pltpu.CompilerParams(
            collective_id=0, has_side_effects=True, vmem_limit_bytes=60 * 1024 * 1024
        ),
    )(dens, mask)
    return jnp.transpose(out, (1, 0, 2))


def solution(mesh):
    placed = (P("blk", None, "layer"), P("blk", None, "layer"))
    return jax.shard_map(
        local, mesh=mesh, in_specs=placed, out_specs=P("blk", None, "layer"), check_vma=False
    )
```

time: 459 us -> 122 us (0.27)
  waiting for transfers between devices: 319 us -> 0 us
  Pallas kernels: 0 us -> 117 us
  blocking collectives: 50.8 us -> 0 us
  matrix products: 41.1 us -> 0 us
  local copies, waits for them, and re-layouts: 20.3 us -> 5.41 us
  between operations: 13.4 us -> 0.01 us
  starting transfers between devices: 8.95 us -> 0 us
    reduce_scatter x1 -> x0, waiting for transfers between devices: 177 us -> none  [local(): lax.psum_scatter(partial_value, 'layer', scatter_dimension=2, tiled=True)]
    ppermute x2 -> x0, waiting for transfers between devices: 142 us -> none  [passed_along(): lax.ppermute(shard, axis, [(i, (i + by) % devices) for i in range(devices)])]
    pallas_call x0 -> x1, Pallas kernels: none -> 117 us  [local(): pl.pallas_call(kernel, out_shape=jax.ShapeDtypeStruct((5, rows, cols), F3...]
    all_to_all x1 -> x0, blocking collectives: 50.8 us -> none  [local(): lax.all_to_all(kept, 'layer', split_axis=0, concat_axis=2, tiled=True)]
    dot_general x3 -> x0, matrix products: 41.1 us -> none  [band_product(): jnp.dot(left[:, offset, :], flat, preferred_element_type=jnp.float32, pre...]
    ppermute x2 -> x0, starting transfers between devices: 8.95 us -> none  [passed_along(): lax.ppermute(shard, axis, [(i, (i + by) % devices) for i in range(devices)])]
    scatter-add x1 -> x0, local copies, waits for them, and re-layouts: 7.81 us -> none  [band_product(): result = result.at[:, offset:offset + 3, :].add(term.reshape(rows, 3, cols))]
    mul x3 -> x0, local copies, waits for them, and re-layouts: 6.67 us -> none  [local(): density.reshape(tile_rows, TILE, 3, tile_cols, TILE)]
  transfers between devices with their start and end apart: 3 -> 0, of which waited for: 3 -> 0; matrix products, arithmetic and copies ran while one was open for 0% -> 0% of each run, Pallas kernels for 0% -> 0%
where the time goes in v1:
time: 122 us
  Pallas kernels  117 us (96%)
  local copies, waits for them, and re-layouts  5.41 us (4%)
    pallas_call x1, Pallas kernels, local(): pl.pallas_call(kernel, out_shape=jax.ShapeDtypeStruct((5, rows, cols), F3...  117 us
    unnamed x1, local copies, waits for them, and re-layouts  5.41 us

profile of v1, /device:TPU:0, one launch (start us, length us, event | category | flops | bytes accessed | tf_op | source)
XLA Modules:
  0.0 122.2 jit_solution(14925752254689609596)
XLA Ops:
  0.0 116.8 %shard_map.28 = f32[5,1024,256]{2,1,0:T(8,128)} custom-call(f32[3,1024,256]{2,1,0:T(8,128)} %bitcast.4, s32[3,2,8]{2,1,0:T(2,128)} %bitcast.5), custom_call_target="tpu_custom_call" | custom-call | tf_op jit(solution)/shard_map/pallas_call | solution.py:247
  116.8 5.4 %copy.4 = f32[1024,5,256]{2,0,1:T(8,128)} copy(f32[1024,5,256]{2,0,1:T(8,128)} %bitcast.3) | data formatting | bytes 10485760

commit v2 on v1

--- a/solution.py
+++ b/solution.py
@@ -9,8 +9,11 @@
 
 TILE = 128
 Q = 256
-SUB = 64
-NSUB = Q // SUB
+PIECES = [[32, 32, 64, 64, 64]] + [[64] * 4] * 10 + [[64, 64, 64, 32, 32]]
+STEPS = [(k, sum(rows[:i]), n, i) for k, rows in enumerate(PIECES) for i, n in enumerate(rows)]
+LAST = [max(s for s, step in enumerate(STEPS) if step[0] == k) for k in range(12)]
+LEFT_LAG, RIGHT_LAG = 2, 7
+BUDGET = 128 * 5
 Y = 4
 F32 = jnp.float32
 BF16 = jnp.bfloat16
@@ -57,9 +60,10 @@
         rows = pl.ds(row_of(rho), Q)
         return remote(own.at[b, rows], sib.at[b, rows], sib_send.at[k], sib_recv.at[k], sibling)
 
-    def to_partner(k, rho, b, s):
-        rows = pl.ds(row_of(rho) + s * SUB, SUB)
-        return remote(own.at[b, rows], par.at[b, rows], par_send.at[k], par_recv.at[k, s], partner)
+    def to_partner(k, offset, n, i):
+        rho, b = BLOCKS[k]
+        rows = pl.ds(row_of(rho) + offset, n)
+        return remote(own.at[b, rows], par.at[b, rows], par_send.at[k], par_recv.at[k, i], partner)
 
     def block_to_next(k, rho, b):
         rows = pl.ds(row_of(rho), Q)
@@ -71,8 +75,9 @@
 
     def send_block(k):
         rho, b = BLOCKS[k]
-        for s in range(NSUB):
-            to_partner(k, rho, b, s).start()
+        for step in STEPS:
+            if step[0] == k:
+                to_partner(*step).start()
 
         @pl.when(jnp.logical_not(at_end))
         def _():
@@ -82,10 +87,10 @@
         def _():
             block_to_prev(k, rho, b).start()
 
-    def forward(k, s):
-        rho, b = BLOCKS[k]
-        rows = pl.ds(par_row_of(rho) + s * SUB, SUB)
-        remote(own.at[b, rows], par.at[b, rows], par_send.at[k], par_recv.at[k, s], partner).wait_recv()
+    def forward(k, offset, n, i):
+        rho, b = BLOCKS[k]
+        rows = pl.ds(par_row_of(rho) + offset, n)
+        remote(own.at[b, rows], par.at[b, rows], par_send.at[k], par_recv.at[k, i], partner).wait_recv()
         remote(par.at[b, rows], fwd.at[b, rows], fwd_send.at[k], fwd_recv.at[k], sibling).start()
 
         @pl.when(at_end)
@@ -133,56 +138,70 @@
         dot = functools.partial(jnp.dot, preferred_element_type=F32)
         out[o + b, rows, :] += dot(ah, wh) + dot(ah, wl) + dot(al, wh)
 
-    def arrive(k):
+    def left_arrives(k):
         rho, b = BLOCKS[k]
         prow = par_row_of(rho)
         rows = pl.ds(prow, Q)
         keep_left(2 + core, b, prow, Q, par[b, rows, :])
         remote(par.at[b, rows], fwd.at[b, rows], fwd_send.at[k], fwd_recv.at[k], sibling).wait_recv()
         keep_left(3 - core, b, prow, Q, fwd[b, rows, :])
-        krows = pl.ds(row_of(rho), Q)
+
+    def right_arrives(k):
+        rho, b = BLOCKS[k]
+        rows = pl.ds(row_of(rho), Q)
         block_to_next(k, rho, b).wait_recv()
-        hi, lo = split(pre[b, krows, :])
+        hi, lo = split(pre[b, rows, :])
         rh[0, rho, b] = hi
         rl[0, rho, b] = lo
         block_to_prev(k, rho, b).wait_recv()
-        hi, lo = split(fol[b, krows, :])
+        hi, lo = split(fol[b, rows, :])
         rh[1, rho, b] = hi
         rl[1, rho, b] = lo
 
+    def sibling_arrives(k):
+        rho, b = BLOCKS[k]
+        to_sibling(k, rho, b).wait_recv()
+        r0 = row_of(rho)
+        keep_left(1 - core, b, r0, Q, sib[b, pl.ds(r0, Q), :])
+
     first = pl.multiple_of((1 - half) * 2 * Q, 2 * Q)
-
-    def work(k):
-        rho, b = BLOCKS[k]
-        third, fourth = par_row_of(2), par_row_of(3)
-        todo = [functools.partial(arrive, k)]
-
-        def add(*what):
-            todo.append(functools.partial(product, *what))
-
-        if rho < 2:
-            for o in (0, 2):
-                add(o, b, rho, 0, 4 * Q)
-        else:
-            for o in (0, 2):
-                have = 3 * (rho - 2) + b - o
-                if have >= 3:
-                    add(o, b, rho, 0, 4 * Q)
-                else:
-                    add(o, b, rho, first, 2 * Q)
-                    if have >= 0:
-                        add(o, b, rho, third, Q)
-            if b != 1:
-                rows = third if rho == 2 else fourth
-                for r in (2, 3):
-                    for c in range(3):
-                        if 3 * r + c < k:
-                            add(b, c, r, rows, Q)
+    queue = []
+
+    def add(when, cost, what, *args):
+        queue.append((min(when, len(STEPS)), cost, functools.partial(what, *args)))
+
+    def add_product(when, *args):
+        add(when, args[-1], product, *args)
+
+    for k in range(12):
+        add(0, Q, sibling_arrives, k)
+    for b in range(3):
+        for rho in range(2):
+            add_product(0, 1, b, rho, 0, 4 * Q)
+    for k, (rho, b) in enumerate(BLOCKS):
+        with_left = LAST[k] + LEFT_LAG
+        with_right = LAST[k] + RIGHT_LAG
+        crossed = LAST[k - 1] + RIGHT_LAG if k else 0
+        rows = par_row_of(rho)
+        add(with_left, 2 * Q, left_arrives, k)
         if b == 1:
             for c in range(3):
                 for r in (2, 3):
-                    add(1, c, r, par_row_of(rho), Q)
-        return todo
+                    add_product(with_left, 1, c, r, rows, Q)
+        elif rho >= 2:
+            for r in (2, 3):
+                for c in range(3):
+                    if 3 * r + c < k:
+                        add_product(max(with_left, crossed), b, c, r, rows, Q)
+        add(with_right, 2 * Q, right_arrives, k)
+        for o in (0, 2):
+            if rho < 2 or 3 * rho + b >= 9 + o:
+                add_product(with_right, o, b, rho, 0, 4 * Q)
+            else:
+                add_product(with_right, o, b, rho, first, 2 * Q)
+                if 3 * rho + b >= 6 + o:
+                    add_product(with_right, o, b, rho, par_row_of(2), Q)
+    queue.sort(key=lambda entry: entry[0])
 
     for k, (rho, b) in enumerate(BLOCKS):
         load(k, rho, b).start()
@@ -203,30 +222,18 @@
     for j in range(5):
         out[j] = jnp.zeros_like(out[j])
 
-    def sib_block(k):
-        rho, b = BLOCKS[k]
-        to_sibling(k, rho, b).wait_recv()
-        rows = pl.ds(row_of(rho), Q)
-        keep_left(1 - core, b, row_of(rho), Q, sib[b, rows, :])
-
-    queue = [(0, functools.partial(sib_block, k)) for k in range(12)]
-    queue += [(0, functools.partial(product, 1, b, r, 0, 4 * Q)) for b in range(3) for r in range(2)]
-    for k in range(12):
-        queue += [(min(NSUB * (k + 1) + 1, 12 * NSUB - 1) if k < 11 else 12 * NSUB, t) for t in work(k)]
-    at = 0
-    for s in range(12 * NSUB):
-        k, piece = divmod(s, NSUB)
-        if piece == 0 and k + 2 < 12:
+    for s, step in enumerate(STEPS):
+        k, _, _, i = step
+        if i == 0 and k + 2 < 12:
             send_block(k + 2)
-        forward(k, piece)
-        done = 0
-        limit = 4 if s < 12 * NSUB - 4 else 3
-        while at < len(queue) and queue[at][0] <= s and done < limit:
-            queue[at][1]()
-            at += 1
-            done += 1
-    for _, thunk in queue[at:]:
-        thunk()
+        forward(*step)
+        spent = 0
+        while queue and queue[0][0] <= s and spent < BUDGET:
+            _, cost, what = queue.pop(0)
+            what()
+            spent += cost
+    for _, _, what in queue:
+        what()
 
     for k, (rho, b) in enumerate(BLOCKS):
         rows = pl.ds(row_of(rho), Q)
@@ -246,17 +253,17 @@
     rows, cols = dens.shape[1:]
     out = pl.pallas_call(
         kernel,
-        out_shape=jax.ShapeDtypeStruct((5, rows, cols), F32),
+        out_shape=pltpu.VMEM((5, rows, cols), F32),
         in_specs=[pl.BlockSpec(memory_space=pl.ANY), pl.BlockSpec(memory_space=pltpu.SMEM)],
         out_specs=pl.BlockSpec(memory_space=pltpu.VMEM),
         scratch_shapes=[panel] * 6
         + [pltpu.VMEM((4, 3, rows, cols), BF16)] * 2
         + [pltpu.VMEM((2, 4, 3, Q, cols), BF16)] * 2
         + [dma((12,))] * 4
-        + [dma((12, NSUB))]
+        + [dma((12, max(map(len, PIECES))))]
         + [dma((12,))] * 6,
         compiler_params=pltpu.CompilerParams(
-            collective_id=0, has_side_effects=True, vmem_limit_bytes=60 * 1024 * 1024
+            collective_id=0, has_side_effects=True, vmem_limit_bytes=50 * 1024 * 1024
         ),
     )(dens, mask)
     return jnp.transpose(out, (1, 0, 2))

time: 122 us -> 87.3 us (0.72)
  Pallas kernels: 117 us -> 84.8 us
  local copies, waits for them, and re-layouts: 5.41 us -> 2.36 us
    pallas_call x1, Pallas kernels: 117 us -> 84.8 us  [local(): pl.pallas_call(kernel, out_shape=pltpu.VMEM((5, rows, cols), F32), in_spe...]
    unnamed x1, local copies, waits for them, and re-layouts: 5.41 us -> 2.36 us
where the time goes in v2:
time: 87.3 us; the launch traced here: 87.1 us
  Pallas kernels  84.8 us (97%)
  local copies, waits for them, and re-layouts  2.36 us (3%)
    pallas_call x1, Pallas kernels, local(): pl.pallas_call(kernel, out_shape=pltpu.VMEM((5, rows, cols), F32), in_spe...  84.8 us
    unnamed x1, local copies, waits for them, and re-layouts  2.36 us

profile of v2, /device:TPU:0, one launch (start us, length us, event | category | flops | bytes accessed | tf_op | source)
XLA Modules:
  0.0 87.1 jit_solution(10162386054185871059)
XLA Ops:
  0.0 84.8 %shard_map.28 = f32[5,1024,256]{2,1,0:T(8,128)S(1)} custom-call(f32[3,1024,256]{2,1,0:T(8,128)} %bitcast.4, s32[3,2,8]{2,1,0:T(2,128)} %bitcast.5), custom_call_target="tpu_custom_call" | custom-call | tf_op jit(solution)/shard_map/pallas_call | solution.py:254
  84.8 2.4 %copy.4 = f32[1024,5,256]{2,0,1:T(8,128)} copy(f32[1024,5,256]{2,0,1:T(8,128)S(1)} %bitcast.3) | data formatting | bytes 10485760

commit v3 on v2

--- a/solution.py
+++ b/solution.py
@@ -9,10 +9,10 @@
 
 TILE = 128
 Q = 256
-PIECES = [[32, 32, 64, 64, 64]] + [[64] * 4] * 10 + [[64, 64, 64, 32, 32]]
+PIECES = [[48, 48, 56, 56, 48]] * 12
 STEPS = [(k, sum(rows[:i]), n, i) for k, rows in enumerate(PIECES) for i, n in enumerate(rows)]
 LAST = [max(s for s, step in enumerate(STEPS) if step[0] == k) for k in range(12)]
-LEFT_LAG, RIGHT_LAG = 2, 7
+LEFT_LAG, RIGHT_LAG = 2, 9
 BUDGET = 128 * 5
 Y = 4
 F32 = jnp.float32
@@ -22,7 +22,7 @@
 
 
 def kernel(
-    dens, mask, out, own, sib, par, fwd, pre, fol, lh, ll, rh, rl,
+    dens, mask, out, lh, ll, last_h, last_l, own, sib, par, fwd, pre, fol, rh, rl,
     load_sem, sib_send, sib_recv, par_send, par_recv, fwd_send, fwd_recv,
     nxt_send, pre_recv, prv_send, fol_recv,
 ):
@@ -149,14 +149,15 @@
     def right_arrives(k):
         rho, b = BLOCKS[k]
         rows = pl.ds(row_of(rho), Q)
-        block_to_next(k, rho, b).wait_recv()
-        hi, lo = split(pre[b, rows, :])
-        rh[0, rho, b] = hi
-        rl[0, rho, b] = lo
-        block_to_prev(k, rho, b).wait_recv()
-        hi, lo = split(fol[b, rows, :])
-        rh[1, rho, b] = hi
-        rl[1, rho, b] = lo
+        for side, copy, panel in ((0, block_to_next, pre), (1, block_to_prev, fol)):
+            copy(k, rho, b).wait_recv()
+            hi, lo = split(panel[b, rows, :])
+            if k < 11:
+                rh[side, rho, b] = hi
+                rl[side, rho, b] = lo
+            else:
+                last_h[side] = hi
+                last_l[side] = lo
 
     def sibling_arrives(k):
         rho, b = BLOCKS[k]
@@ -194,7 +195,7 @@
                     if 3 * r + c < k:
                         add_product(max(with_left, crossed), b, c, r, rows, Q)
         add(with_right, 2 * Q, right_arrives, k)
-        for o in (0, 2):
+        for o in (0, 2) if k < 11 else ():
             if rho < 2 or 3 * rho + b >= 9 + o:
                 add_product(with_right, o, b, rho, 0, 4 * Q)
             else:
@@ -245,27 +246,53 @@
         block_to_prev(k, rho, b).wait_send()
 
 
+def finish(acc, lh, ll, last_h, last_l, out, done, sem):
+    def write(src, j):
+        return pltpu.make_async_copy(src, out.at[j], sem.at[j])
+
+    for j in (0, 1, 3):
+        write(acc.at[j], j).start()
+    dot = functools.partial(jnp.dot, preferred_element_type=F32)
+    for side, o in enumerate((0, 2)):
+        ah, al, wh, wl = lh[3, o], ll[3, o], last_h[side], last_l[side]
+        done[side] = acc[o + 2] + (dot(ah, wh) + dot(ah, wl) + dot(al, wh))
+        write(done.at[side], o + 2).start()
+    for j in range(5):
+        write(acc.at[j], j).wait()
+
+
 def local(density, tile_mask):
     dens = jnp.transpose(density, (1, 0, 2))
     mask = jnp.transpose(tile_mask, (1, 2, 0))
     panel = pltpu.VMEM(dens.shape, F32)
     dma = pltpu.SemaphoreType.DMA
     rows, cols = dens.shape[1:]
-    out = pl.pallas_call(
+    left = pltpu.VMEM((4, 3, rows, cols), BF16)
+    last = pltpu.VMEM((2, Q, cols), BF16)
+    in_vmem = pl.BlockSpec(memory_space=pltpu.VMEM)
+    held = pl.pallas_call(
         kernel,
-        out_shape=pltpu.VMEM((5, rows, cols), F32),
+        out_shape=(pltpu.VMEM((5, rows, cols), F32), left, left, last, last),
         in_specs=[pl.BlockSpec(memory_space=pl.ANY), pl.BlockSpec(memory_space=pltpu.SMEM)],
-        out_specs=pl.BlockSpec(memory_space=pltpu.VMEM),
+        out_specs=(in_vmem,) * 5,
         scratch_shapes=[panel] * 6
-        + [pltpu.VMEM((4, 3, rows, cols), BF16)] * 2
         + [pltpu.VMEM((2, 4, 3, Q, cols), BF16)] * 2
         + [dma((12,))] * 4
         + [dma((12, max(map(len, PIECES))))]
         + [dma((12,))] * 6,
         compiler_params=pltpu.CompilerParams(
-            collective_id=0, has_side_effects=True, vmem_limit_bytes=50 * 1024 * 1024
+            collective_id=0, has_side_effects=True, vmem_limit_bytes=40 * 1024 * 1024
         ),
     )(dens, mask)
+    held = [pltpu.with_memory_space_constraint(x, pltpu.VMEM) for x in held]
+    out = pl.pallas_call(
+        finish,
+        out_shape=jax.ShapeDtypeStruct((5, rows, cols), F32),
+        in_specs=[in_vmem] * 5,
+        out_specs=pl.BlockSpec(memory_space=pl.ANY),
+        scratch_shapes=[pltpu.VMEM((2, rows, cols), F32), dma((5,))],
+        compiler_params=pltpu.CompilerParams(vmem_limit_bytes=5 * 1024 * 1024),
+    )(*held)
     return jnp.transpose(out, (1, 0, 2))
 
 

time: 87.3 us -> 86.4 us (0.990)
  local copies, waits for them, and re-layouts: 2.36 us -> 0 us
  Pallas kernels: 84.8 us -> 86.1 us
    unnamed x1 -> x0, local copies, waits for them, and re-layouts: 2.36 us -> none
    pallas_call x1 -> x2, Pallas kernels: 84.8 us -> 86.1 us  [the longest x1 83.7 us: local(): pl.pallas_call(kernel, out_shape=(pltpu.VMEM((5, rows, cols), F32), left,...]
where the time goes in v3:
time: 86.4 us; the launch traced here: 86.3 us
  Pallas kernels  86.1 us (100%)
    pallas_call x1, Pallas kernels, local(): pl.pallas_call(kernel, out_shape=(pltpu.VMEM((5, rows, cols), F32), left,...  83.7 us
    pallas_call x1, Pallas kernels, local(): pl.pallas_call(finish, out_shape=jax.ShapeDtypeStruct((5, rows, cols), F3...  2.41 us

profile of v3, /device:TPU:0, one launch (start us, length us, event | category | flops | bytes accessed | tf_op | source)
XLA Modules:
  0.0 86.3 jit_solution(15270081313538816567)
XLA Ops:
  0.0 83.7 %shard_map.28 = (f32[5,1024,256]{2,1,0:T(8,128)S(1)}, bf16[4,3,1024,256]{3,2,1,0:T(8,128)(2,1)S(1)}, bf16[4,3,1024,256]{3,2,1,0:T(8,128)(2,1)S(1)}, bf16[2,256,2...) custom-call(f32[3,1024,256]{2,1,0:T(8,128)} %bitcast.3, s32[3,2,8]{2,1,0:T(2,128)} %bitcast.4), custom_call_target="tpu_custom_call" | custom-call | tf_op jit(solution)/shard_map/pallas_call | solution.py:273
  83.7 2.4 %shard_map.29 = f32[5,1024,256]{2,1,0:T(8,128)} custom-call(f32[5,1024,256]{2,1,0:T(8,128)S(1)} %get-tuple-element.10.acc, bf16[4,3,1024,256]{3,2,1,0:T(8,128)(2,1)S(1)} %get-tuple-element.11.lh, bf16[4,3,1024,256]{3,2,1,0:T(8,128)(2,1)S(1)} %get-tuple-element.12.ll, bf16[2,256,256]{2,1,0:T(8,128)(2,1)S(1)} %get-tuple-element.13.last_h, ...), custom_call_target="tpu_custom_call" | custom-call | tf_op jit(solution)/shard_map/pallas_call | solution.py:288

commit v4 on v3

--- a/solution.py
+++ b/solution.py
@@ -9,9 +9,11 @@
 
 TILE = 128
 Q = 256
-PIECES = [[48, 48, 56, 56, 48]] * 12
+PIECES = [[48, 48, 56, 56, 48]] * 11 + [[48, 56, 56, 48, 48]]
 STEPS = [(k, sum(rows[:i]), n, i) for k, rows in enumerate(PIECES) for i, n in enumerate(rows)]
 LAST = [max(s for s, step in enumerate(STEPS) if step[0] == k) for k in range(12)]
+LATE = 96
+LATE_AFTER, RELAY_AFTER, PASS_AFTER = 5, 7, 9
 LEFT_LAG, RIGHT_LAG = 2, 9
 BUDGET = 128 * 5
 Y = 4
@@ -22,9 +24,9 @@
 
 
 def kernel(
-    dens, mask, out, lh, ll, last_h, last_l, own, sib, par, fwd, pre, fol, rh, rl,
+    dens, mask, out, lh, ll, last_h, last_l, own, sib, par, fwd, pre, fol, rh, rl, transit,
     load_sem, sib_send, sib_recv, par_send, par_recv, fwd_send, fwd_recv,
-    nxt_send, pre_recv, prv_send, fol_recv,
+    nxt_send, pre_recv, prv_send, fol_recv, late_send, late_recv, relay_send, relay_recv, far_ok,
 ):
     blk = lax.axis_index("blk")
     lay = lax.axis_index("layer")
@@ -40,6 +42,8 @@
     nxt = (lax.rem(blk + 1, nblk), jnp.where(at_end, other_half, lay))
     prv = (lax.rem(blk + nblk - 1, nblk), jnp.where(at_start, other_half, lay))
 
+    beyond = (lax.rem(blk + jnp.where(y == 1, nblk - 3, 3), nblk), lay)
+
     def row_of(rho):
         return pl.multiple_of(lax.rem(2 * half + rho, 4) * Q, Q)
 
@@ -65,13 +69,86 @@
         rows = pl.ds(row_of(rho) + offset, n)
         return remote(own.at[b, rows], par.at[b, rows], par_send.at[k], par_recv.at[k, i], partner)
 
+    def panel_rows(k, rho):
+        return pl.ds(row_of(rho), Q if k < 11 else Q - LATE)
+
     def block_to_next(k, rho, b):
-        rows = pl.ds(row_of(rho), Q)
+        rows = panel_rows(k, rho)
         return remote(own.at[b, rows], pre.at[b, rows], nxt_send.at[k], pre_recv.at[k], nxt)
 
     def block_to_prev(k, rho, b):
-        rows = pl.ds(row_of(rho), Q)
+        rows = panel_rows(k, rho)
         return remote(own.at[b, rows], fol.at[b, rows], prv_send.at[k], fol_recv.at[k], prv)
+
+    late = (2, pl.ds(row_of(3) + Q - LATE, LATE))
+
+    def late_to_next():
+        return remote(own.at[late], pre.at[late], late_send.at[0], late_recv.at[0], nxt)
+
+    def late_to_prev():
+        return remote(own.at[late], fol.at[late], late_send.at[1], late_recv.at[1], prv)
+
+    def late_across(panel):
+        return remote(panel.at[late], transit, relay_send.at[0], relay_recv.at[0], beyond)
+
+    def late_on(panel, recv, to):
+        return remote(transit, panel.at[late], relay_send.at[1], recv, to)
+
+    def send_late():
+        @pl.when(jnp.logical_not(at_end))
+        def _():
+            late_to_next().start()
+
+        @pl.when(jnp.logical_not(at_start))
+        def _():
+            late_to_prev().start()
+
+    def relay_late():
+        @pl.when(y == 2)
+        def _():
+            late_to_prev().wait_recv()
+            late_across(fol).start()
+
+        @pl.when(y == 1)
+        def _():
+            late_to_next().wait_recv()
+            late_across(pre).start()
+
+    def pass_late():
+        @pl.when((y == 1) | (y == 2))
+        def _():
+            late_across(fol).wait_recv()
+
+        @pl.when(y == 1)
+        def _():
+            late_on(pre, late_recv.at[0], prv).start()
+
+        @pl.when(y == 2)
+        def _():
+            late_on(fol, late_recv.at[1], nxt).start()
+
+    def late_arrives():
+        @pl.when(y != 1)
+        def _():
+            late_to_next().wait_recv()
+
+        @pl.when(y != 2)
+        def _():
+            late_to_prev().wait_recv()
+
+    def late_sent():
+        @pl.when(jnp.logical_not(at_end))
+        def _():
+            late_to_next().wait_send()
+
+        @pl.when(jnp.logical_not(at_start))
+        def _():
+            late_to_prev().wait_send()
+
+        @pl.when((y == 1) | (y == 2))
+        def _():
+            late_across(fol).wait_send()
+            late_on(fol, late_recv.at[1], nxt).wait_send()
 
     def send_block(k):
         rho, b = BLOCKS[k]
@@ -93,12 +170,17 @@
         remote(own.at[b, rows], par.at[b, rows], par_send.at[k], par_recv.at[k, i], partner).wait_recv()
         remote(par.at[b, rows], fwd.at[b, rows], fwd_send.at[k], fwd_recv.at[k], sibling).start()
 
+        if k == 11 and offset >= Q - LATE:
+            return
+
         @pl.when(at_end)
         def _():
             remote(par.at[b, rows], pre.at[b, rows], nxt_send.at[k], pre_recv.at[k], nxt).start()
 
         @pl.when(at_start)
         def _():
+            if k == 0 and i == 0:
+                pl.semaphore_wait(far_ok, 1)
             remote(par.at[b, rows], fol.at[b, rows], prv_send.at[k], fol_recv.at[k], prv).start()
 
     def split(x):
@@ -148,6 +230,8 @@
 
     def right_arrives(k):
         rho, b = BLOCKS[k]
+        if k == 11:
+            late_arrives()
         rows = pl.ds(row_of(rho), Q)
         for side, copy, panel in ((0, block_to_next, pre), (1, block_to_prev, fol)):
             copy(k, rho, b).wait_recv()
@@ -207,12 +291,28 @@
     for k, (rho, b) in enumerate(BLOCKS):
         load(k, rho, b).start()
     barrier = pltpu.get_barrier_semaphore()
-    for device in (partner, sibling, nxt, prv):
+    for device in (partner, sibling, prv):
         pl.semaphore_signal(barrier, inc=1, device_id=device, device_id_type=MESH)
+
+    @pl.when(jnp.logical_not(at_end))
+    def _():
+        pl.semaphore_signal(barrier, inc=1, device_id=nxt, device_id_type=MESH)
+
     for k in range(2):
         load(k, *BLOCKS[k]).wait()
         mask_own(*BLOCKS[k])
-    pl.semaphore_wait(barrier, 4)
+    @pl.when(at_start)
+    def _():
+        pl.semaphore_wait(barrier, 3)
+
+    @pl.when(jnp.logical_not(at_start))
+    def _():
+        pl.semaphore_wait(barrier, 4)
+
+    @pl.when(at_end)
+    def _():
+        pl.semaphore_signal(far_ok, inc=1, device_id=nxt, device_id_type=MESH)
+
     for k in range(2):
         send_block(k)
         to_sibling(k, *BLOCKS[k]).start()
@@ -228,6 +328,12 @@
         if i == 0 and k + 2 < 12:
             send_block(k + 2)
         forward(*step)
+        if s == LAST[LATE_AFTER]:
+            send_late()
+        if s == LAST[RELAY_AFTER]:
+            relay_late()
+        if s == LAST[PASS_AFTER]:
+            pass_late()
         spent = 0
         while queue and queue[0][0] <= s and spent < BUDGET:
             _, cost, what = queue.pop(0)
@@ -236,6 +342,7 @@
     for _, _, what in queue:
         what()
 
+    late_sent()
     for k, (rho, b) in enumerate(BLOCKS):
         rows = pl.ds(row_of(rho), Q)
         prow = pl.ds(par_row_of(rho), Q)
@@ -277,9 +384,12 @@
         out_specs=(in_vmem,) * 5,
         scratch_shapes=[panel] * 6
         + [pltpu.VMEM((2, 4, 3, Q, cols), BF16)] * 2
+        + [pltpu.VMEM((LATE, cols), F32)]
         + [dma((12,))] * 4
         + [dma((12, max(map(len, PIECES))))]
-        + [dma((12,))] * 6,
+        + [dma((12,))] * 6
+        + [dma((2,))] * 3
+        + [dma((1,)), pltpu.SemaphoreType.REGULAR],
         compiler_params=pltpu.CompilerParams(
             collective_id=0, has_side_effects=True, vmem_limit_bytes=40 * 1024 * 1024
         ),

time: 86.4 us -> 85.1 us (0.985)
  Pallas kernels: 86.1 us -> 84.8 us
    pallas_call x1, Pallas kernels: 83.7 us -> 82.4 us  [local(): pl.pallas_call(kernel, out_shape=(pltpu.VMEM((5, rows, cols), F32), left,...]
where the time goes in v4:
time: 85.1 us; the launch traced here: 85 us
  Pallas kernels  84.8 us (100%)
    pallas_call x1, Pallas kernels, local(): pl.pallas_call(kernel, out_shape=(pltpu.VMEM((5, rows, cols), F32), left,...  82.4 us
    pallas_call x1, Pallas kernels, local(): pl.pallas_call(finish, out_shape=jax.ShapeDtypeStruct((5, rows, cols), F3...  2.41 us

profile of v4, /device:TPU:0, one launch (start us, length us, event | category | flops | bytes accessed | tf_op | source)
XLA Modules:
  0.0 85.0 jit_solution(16643442926285821644)
XLA Ops:
  0.0 82.4 %shard_map.28 = (f32[5,1024,256]{2,1,0:T(8,128)S(1)}, bf16[4,3,1024,256]{3,2,1,0:T(8,128)(2,1)S(1)}, bf16[4,3,1024,256]{3,2,1,0:T(8,128)(2,1)S(1)}, bf16[2,256,2...) custom-call(f32[3,1024,256]{2,1,0:T(8,128)} %bitcast.3, s32[3,2,8]{2,1,0:T(2,128)} %bitcast.4), custom_call_target="tpu_custom_call" | custom-call | tf_op jit(solution)/shard_map/pallas_call | solution.py:380
  82.4 2.4 %shard_map.29 = f32[5,1024,256]{2,1,0:T(8,128)} custom-call(f32[5,1024,256]{2,1,0:T(8,128)S(1)} %get-tuple-element.10.acc, bf16[4,3,1024,256]{3,2,1,0:T(8,128)(2,1)S(1)} %get-tuple-element.11.lh, bf16[4,3,1024,256]{3,2,1,0:T(8,128)(2,1)S(1)} %get-tuple-element.12.ll, bf16[2,256,256]{2,1,0:T(8,128)(2,1)S(1)} %get-tuple-element.13.last_h, ...), custom_call_target="tpu_custom_call" | custom-call | tf_op jit(solution)/shard_map/pallas_call | solution.py:398

commit v5 on v4

--- a/solution.py
+++ b/solution.py
@@ -9,10 +9,10 @@
 
 TILE = 128
 Q = 256
-PIECES = [[48, 48, 56, 56, 48]] * 11 + [[48, 56, 56, 48, 48]]
+PIECES = [[48, 48, 56, 56, 48]] * 11 + [[48, 48, 64, 64, 32]]
 STEPS = [(k, sum(rows[:i]), n, i) for k, rows in enumerate(PIECES) for i, n in enumerate(rows)]
 LAST = [max(s for s, step in enumerate(STEPS) if step[0] == k) for k in range(12)]
-LATE = 96
+LATE = 160
 LATE_AFTER, RELAY_AFTER, PASS_AFTER = 5, 7, 9
 LEFT_LAG, RIGHT_LAG = 2, 9
 BUDGET = 128 * 5

time: 85.1 us -> 83.8 us (0.985)
  Pallas kernels: 84.8 us -> 83.5 us
    pallas_call x1, Pallas kernels: 82.4 us -> 81.1 us  [local(): pl.pallas_call(kernel, out_shape=(pltpu.VMEM((5, rows, cols), F32), left,...]
where the time goes in v5:
time: 83.8 us; the launch traced here: 83.6 us
  Pallas kernels  83.5 us (100%)
    pallas_call x1, Pallas kernels, local(): pl.pallas_call(kernel, out_shape=(pltpu.VMEM((5, rows, cols), F32), left,...  81.1 us
    pallas_call x1, Pallas kernels, local(): pl.pallas_call(finish, out_shape=jax.ShapeDtypeStruct((5, rows, cols), F3...  2.41 us

profile of v5, /device:TPU:0, one launch (start us, length us, event | category | flops | bytes accessed | tf_op | source)
XLA Modules:
  0.0 83.6 jit_solution(18250508049528228313)
XLA Ops:
  0.0 81.1 %shard_map.28 = (f32[5,1024,256]{2,1,0:T(8,128)S(1)}, bf16[4,3,1024,256]{3,2,1,0:T(8,128)(2,1)S(1)}, bf16[4,3,1024,256]{3,2,1,0:T(8,128)(2,1)S(1)}, bf16[2,256,2...) custom-call(f32[3,1024,256]{2,1,0:T(8,128)} %bitcast.3, s32[3,2,8]{2,1,0:T(2,128)} %bitcast.4), custom_call_target="tpu_custom_call" | custom-call | tf_op jit(solution)/shard_map/pallas_call | solution.py:380
  81.1 2.4 %shard_map.29 = f32[5,1024,256]{2,1,0:T(8,128)} custom-call(f32[5,1024,256]{2,1,0:T(8,128)S(1)} %get-tuple-element.10.acc, bf16[4,3,1024,256]{3,2,1,0:T(8,128)(2,1)S(1)} %get-tuple-element.11.lh, bf16[4,3,1024,256]{3,2,1,0:T(8,128)(2,1)S(1)} %get-tuple-element.12.ll, bf16[2,256,256]{2,1,0:T(8,128)(2,1)S(1)} %get-tuple-element.13.last_h, ...), custom_call_target="tpu_custom_call" | custom-call | tf_op jit(solution)/shard_map/pallas_call | solution.py:398

commit v6 on v5

--- a/solution.py
+++ b/solution.py
@@ -9,7 +9,7 @@
 
 TILE = 128
 Q = 256
-PIECES = [[48, 48, 56, 56, 48]] * 11 + [[48, 48, 64, 64, 32]]
+PIECES = [[48, 48, 56, 56, 48]] * 11 + [[32, 32, 32, 64, 96]]
 STEPS = [(k, sum(rows[:i]), n, i) for k, rows in enumerate(PIECES) for i, n in enumerate(rows)]
 LAST = [max(s for s, step in enumerate(STEPS) if step[0] == k) for k in range(12)]
 LATE = 160

time: 83.8 us -> 83.5 us (level)
  no operation moved by 1% of the time
where the time goes in v6:
time: 83.5 us; the launch traced here: 83.3 us
  Pallas kernels  83.2 us (100%)
    pallas_call x1, Pallas kernels, local(): pl.pallas_call(kernel, out_shape=(pltpu.VMEM((5, rows, cols), F32), left,...  80.7 us
    pallas_call x1, Pallas kernels, local(): pl.pallas_call(finish, out_shape=jax.ShapeDtypeStruct((5, rows, cols), F3...  2.41 us

profile of v6, /device:TPU:0, one launch (start us, length us, event | category | flops | bytes accessed | tf_op | source)
XLA Modules:
  0.0 83.3 jit_solution(6676881015604636351)
XLA Ops:
  0.0 80.7 %shard_map.28 = (f32[5,1024,256]{2,1,0:T(8,128)S(1)}, bf16[4,3,1024,256]{3,2,1,0:T(8,128)(2,1)S(1)}, bf16[4,3,1024,256]{3,2,1,0:T(8,128)(2,1)S(1)}, bf16[2,256,2...) custom-call(f32[3,1024,256]{2,1,0:T(8,128)} %bitcast.3, s32[3,2,8]{2,1,0:T(2,128)} %bitcast.4), custom_call_target="tpu_custom_call" | custom-call | tf_op jit(solution)/shard_map/pallas_call | solution.py:380
  80.7 2.4 %shard_map.29 = f32[5,1024,256]{2,1,0:T(8,128)} custom-call(f32[5,1024,256]{2,1,0:T(8,128)S(1)} %get-tuple-element.10.acc, bf16[4,3,1024,256]{3,2,1,0:T(8,128)(2,1)S(1)} %get-tuple-element.11.lh, bf16[4,3,1024,256]{3,2,1,0:T(8,128)(2,1)S(1)} %get-tuple-element.12.ll, bf16[2,256,256]{2,1,0:T(8,128)(2,1)S(1)} %get-tuple-element.13.last_h, ...), custom_call_target="tpu_custom_call" | custom-call | tf_op jit(solution)/shard_map/pallas_call | solution.py:398
